TPU v7x, 32 devices: a whole 2x2x4 slice. The times are simulated.
32 devices in a mesh: chan: 8 (over z, y), win: 4 (over x, core).
Axes of the slice: x: 2, y: 2, z: 4, core: 2. Of those that a mesh axis runs over, the one named last changes fastest.
Arguments:
- spec_re: bfloat16 [8, 128, 5120], P(None, 'win', 'chan'), may hold values from -6 to 6
- spec_im: bfloat16 [8, 128, 5120], P(None, 'win', 'chan'), may hold values from -6 to 6
- valid: int32 [128, 5120], P('win', 'chan'), may hold values from 0 to 1, as said below
Outputs:
- stack_re: float32 [8, 5120, 5120], P(None, 'chan', 'win')
- stack_im: float32 [8, 5120, 5120], P(None, 'chan', 'win')
Inputs may be any that keep to these rules, and one draw needn't show every extreme that they name: `valid`: each entry is 0 or 1; some channels are 0 in every window.
All inputs are finite; a program needn't handle non-finite values.
Results may differ from a plain program's by a relative error of at most 0.012.
Values may be sent and summed in bfloat16 or wider, within the bound.
A program may use at most 384 MiB of HBM per device.

v0:
```python
import jax
import jax.numpy as jnp
from jax import lax
from jax.sharding import PartitionSpec as P

water_level = 1.0


def shifted(array, axis, by):
    count = lax.axis_size(axis)
    return lax.ppermute(array, axis, [(i, (i + by) % count) for i in range(count)])


def forward(piece):
    return shifted((piece[0], piece[1]), "chan", 1)


def on_device(spec_re, spec_im, valid):
    mask = valid.astype(jnp.float32)
    real_part = spec_re.astype(jnp.float32)
    imag_part = spec_im.astype(jnp.float32)
    amp = jnp.sqrt(real_part * real_part + imag_part * imag_part)
    factor = mask[None] / jnp.maximum(amp, water_level)
    white_re = (real_part * factor).astype(jnp.bfloat16)
    white_im = (imag_part * factor).astype(jnp.bfloat16)
    blocks = lax.axis_size("chan")
    width = spec_re.shape[2]
    bins = spec_re.shape[0]
    mine = lax.axis_index("chan")
    right = jnp.concatenate([white_re, white_im], 1)
    left = jnp.concatenate([right, jnp.concatenate([white_im, -white_re], 1)], 2)

    def accumulate(parts, piece, source):
        data, block_mask = piece
        product = jnp.einsum("fwk,fwc->fkc", left, data, preferred_element_type=jnp.float32)
        pairs = jnp.dot(mask.T, block_mask.astype(jnp.float32), precision=lax.Precision.HIGHEST)
        new_re = lax.dynamic_update_index_in_dim(parts[0], product[:, :width], source, 0)
        new_im = lax.dynamic_update_index_in_dim(parts[1], product[:, width:], source, 0)
        new_count = lax.dynamic_update_index_in_dim(parts[2], pairs, source, 0)
        return (new_re, new_im, new_count)

    parts = (
        jnp.zeros((blocks, bins, width, width), jnp.float32),
        jnp.zeros((blocks, bins, width, width), jnp.float32),
        jnp.zeros((blocks, width, width), jnp.float32),
    )
    parts = accumulate(parts, (right, valid), mine)

    def turn_ahead(step, carry):
        held, ahead = carry
        ahead = forward(ahead)
        held = accumulate(held, ahead, (mine - step) % blocks)
        return (held, ahead)

    parts, ahead = lax.fori_loop(1, blocks, turn_ahead, (parts, (right, valid)))
    summed_re, summed_im, summed_count = (
        lax.psum_scatter(
            parts[0].astype(jnp.bfloat16), "win", scatter_dimension=0, tiled=True
        ).astype(jnp.float32),
        lax.psum_scatter(
            parts[1].astype(jnp.bfloat16), "win", scatter_dimension=0, tiled=True
        ).astype(jnp.float32),
        lax.psum_scatter(
            parts[2].astype(jnp.bfloat16), "win", scatter_dimension=0, tiled=True
        ).astype(jnp.float32),
    )
    owned = summed_re.shape[0]
    denom = jnp.maximum(jnp.transpose(summed_count, (1, 0, 2)).reshape(width, owned * width), 1.0)[
        None
    ]
    flat_re = jnp.transpose(summed_re, (1, 2, 0, 3)).reshape(bins, width, owned * width)
    flat_im = jnp.transpose(summed_im, (1, 2, 0, 3)).reshape(bins, width, owned * width)
    return (flat_re / denom, flat_im / denom)


def solution(mesh):
    in_specs = (P(None, "win", "chan"), P(None, "win", "chan"), P("win", "chan"))
    out_specs = (P(None, "chan", "win"), P(None, "chan", "win"))
    return jax.shard_map(
        on_device, mesh=mesh, in_specs=in_specs, out_specs=out_specs, check_vma=False
    )
```

profile of v0, /device:TPU:3, one launch (start us, length us, event | category | flops | bytes accessed | tf_op | source)
XLA Modules:
  0.0 1175.7 jit_solution(15039723881448306246)
XLA Ops:
  11.2 6.9 fusion.12
  23.8 18.9 %broadcast.13.clone = bf16[8,8,640,640]{3,2,1,0:T(8,128)(2,1)} broadcast(bf16[]{:T(256)} %constant.97), dimensions={} | broadcast | bytes 52428800 | tf_op jit(solution)/shard_map/broadcast.1
  46.0 17.1 %broadcast.13.clone.1 = bf16[8,8,640,640]{3,2,1,0:T(8,128)(2,1)} broadcast(bf16[]{:T(256)} %constant.97), dimensions={} | broadcast | bytes 52428800 | tf_op jit(solution)/shard_map/broadcast.1
  66.4 261.2 %while.23 = (s32[]{:T(128)}, bf16[8,8,640,640]{3,2,1,0:T(8,128)(2,1)}, bf16[8,8,640,640]{3,2,1,0:T(8,128)(2,1)}, bf16[8,640,640]{2,1,0:T(8,128)(2,1)}, bf16[8,64...) while((s32[]{:T(128)}, ...), condition=%wide.region_1.2_spmd, body=%wide.region_0.1_spmd.sunk | while | flops 996167680 | bytes 47513968 | solution.py:55
  68.9 17.7 %collective-permute-done.1 = s32[32,640]{1,0:T(8,128)S(1)} collective-permute-done((s32[32,640]{1,0:T(8,128)S(1)}, s32[32,640]{1,0:T(8,128)S(1)}, u32[]{:S(2)}, u32[]{:S(2)}) %collective-permute-start.1) | collective-permute-done | bytes 81952 | tf_op jit(solution)/shard_map/while/body/eval_jaxpr/ppermute | solution.py:11
  89.0 6.9 fusion.29
  95.8 10.6 fusion.30
  107.1 18.7 %collective-permute-done.1 = s32[32,640]{1,0:T(8,128)S(1)} collective-permute-done((s32[32,640]{1,0:T(8,128)S(1)}, s32[32,640]{1,0:T(8,128)S(1)}, u32[]{:S(2)}, u32[]{:S(2)}) %collective-permute-start.1) | collective-permute-done | bytes 81952 | tf_op jit(solution)/shard_map/while/body/eval_jaxpr/ppermute | solution.py:11
  128.2 6.9 fusion.29
  135.0 10.6 fusion.30
  145.8 18.2 %collective-permute-done.1 = s32[32,640]{1,0:T(8,128)S(1)} collective-permute-done((s32[32,640]{1,0:T(8,128)S(1)}, s32[32,640]{1,0:T(8,128)S(1)}, u32[]{:S(2)}, u32[]{:S(2)}) %collective-permute-start.1) | collective-permute-done | bytes 81952 | tf_op jit(solution)/shard_map/while/body/eval_jaxpr/ppermute | solution.py:11
  166.4 6.9 fusion.29
  173.3 10.5 fusion.30
  184.0 17.3 %collective-permute-done.1 = s32[32,640]{1,0:T(8,128)S(1)} collective-permute-done((s32[32,640]{1,0:T(8,128)S(1)}, s32[32,640]{1,0:T(8,128)S(1)}, u32[]{:S(2)}, u32[]{:S(2)}) %collective-permute-start.1) | collective-permute-done | bytes 81952 | tf_op jit(solution)/shard_map/while/body/eval_jaxpr/ppermute | solution.py:11
  203.7 6.9 fusion.29
  210.6 10.5 fusion.30
  221.3 16.4 %collective-permute-done.1 = s32[32,640]{1,0:T(8,128)S(1)} collective-permute-done((s32[32,640]{1,0:T(8,128)S(1)}, s32[32,640]{1,0:T(8,128)S(1)}, u32[]{:S(2)}, u32[]{:S(2)}) %collective-permute-start.1) | collective-permute-done | bytes 81952 | tf_op jit(solution)/shard_map/while/body/eval_jaxpr/ppermute | solution.py:11
  240.0 6.9 fusion.29
  246.9 10.6 fusion.30
  257.7 15.4 %collective-permute-done.1 = s32[32,640]{1,0:T(8,128)S(1)} collective-permute-done((s32[32,640]{1,0:T(8,128)S(1)}, s32[32,640]{1,0:T(8,128)S(1)}, u32[]{:S(2)}, u32[]{:S(2)}) %collective-permute-start.1) | collective-permute-done | bytes 81952 | tf_op jit(solution)/shard_map/while/body/eval_jaxpr/ppermute | solution.py:11
  275.5 6.9 fusion.29
  282.4 10.6 fusion.30
  293.2 14.5 %collective-permute-done.1 = s32[32,640]{1,0:T(8,128)S(1)} collective-permute-done((s32[32,640]{1,0:T(8,128)S(1)}, s32[32,640]{1,0:T(8,128)S(1)}, u32[]{:S(2)}, u32[]{:S(2)}) %collective-permute-start.1) | collective-permute-done | bytes 81952 | tf_op jit(solution)/shard_map/while/body/eval_jaxpr/ppermute | solution.py:11
  310.1 6.9 fusion.29
  316.9 10.6 fusion.30
  327.6 9.5 copy.8
  338.6 61.3 %reduce-scatter.6.cloned.1.call-done = bf16[2,640,640]{1,2,0:T(8,128)(2,1)} async-done(((bf16[8,640,640]{1,2,0:T(8,128)(2,1)}), bf16[2,640,640]{1,2,0:T(8,128)(2,1)}) %reduce-scatter.6.cloned.1.call-update) | async-done | bytes 1638416 | tf_op jit(solution)/shard_map/reduce_scatter | solution.py:63
  404.6 355.0 %reduce-scatter.8.cloned.1.call-done = bf16[2,8,640,640]{3,2,1,0:T(8,128)(2,1)} async-done(((bf16[8,8,640,640]{3,2,1,0:T(8,128)(2,1)}), bf16[2,8,640,640]{3,2,1,0:T(8,128)(2,1)}) %reduce-scatter.8.cloned.1.call-update) | async-done | bytes 13107216 | tf_op jit(solution)/shard_map/reduce_scatter | solution.py:60
  766.3 13.6 %copy.12 = f32[2,8,80,8,640]{4,3,0,2,1:T(8,128)} copy(f32[2,8,80,8,640]{4,3,2,1,0:T(8,128)S(1)} %convert_bitcast_fusion) | data formatting | bytes 52428800 | tf_op jit(solution)/shard_map/reshape | solution.py:72
  779.9 339.1 %reduce-scatter.4.cloned.1.call-done = bf16[2,8,640,640]{3,2,1,0:T(8,128)(2,1)} async-done(((bf16[8,8,640,640]{3,2,1,0:T(8,128)(2,1)}), bf16[2,8,640,640]{3,2,1,0:T(8,128)(2,1)}) %reduce-scatter.4.cloned.1.call-update) | async-done | bytes 13107216 | tf_op jit(solution)/shard_map/reduce_scatter | solution.py:57
  1125.8 9.2 copy.11
  1135.0 34.2 %broadcast_divide_fusion = (f32[8,640,1280]{2,1,0:T(8,128)}, f32[8,640,1280]{2,1,0:T(8,128)}) fusion(f32[8,640,1280]{2,1,0:T(8,128)} %bitcast.44, f32[640,1280]{1,0:T(8,128)S(1)} %copy-done, f32[8,640,1280]{2,1,0:T(8,128)} %bitcast.45), kind=kLoop, calls=%fused_computation.12 | loop fusion | flops 13107200 | bytes 108134400 | tf_op jit(solution)/shard_map/div | solution.py:73
  (73 shorter events, 56.7 us)
Async XLA Ops:
  7.2 392.8 %reduce-scatter.6.cloned.1.call-start = ((), (), s32[]{:S(2)}) async-start(), calls=%async_computation.4 | async-start | bytes 8192000 | tf_op jit(solution)/shard_map/reduce_scatter | solution.py:63
  21.4 21.3 %slice-start = ((s8[13107200]{0:T(1024)(128)(4,1)}), s8[4194304]{0:T(1024)(128)(4,1)S(1)}, s32[]{:S(2)}) async-start(s8[13107200]{0:T(1024)(128)(4,1)} %bitcast.46), calls=%async_computation.6 | async-start | bytes 8388608
  23.8 19.0 %slice-start.1 = ((s8[13107200]{0:T(1024)(128)(4,1)}), s8[4194304]{0:T(1024)(128)(4,1)S(1)}, s32[]{:S(2)}) async-start(s8[13107200]{0:T(1024)(128)(4,1)} %bitcast.46), calls=%async_computation.7 | async-start | bytes 8388608
  23.8 19.0 %slice-start.2 = ((s8[13107200]{0:T(1024)(128)(4,1)}), s8[4194304]{0:T(1024)(128)(4,1)S(1)}, s32[]{:S(2)}) async-start(s8[13107200]{0:T(1024)(128)(4,1)} %bitcast.46), calls=%async_computation.8 | async-start | bytes 8388608
  23.8 19.0 %slice-start.3 = ((s8[13107200]{0:T(1024)(128)(4,1)}), s8[524288]{0:T(1024)(128)(4,1)S(1)}, s32[]{:S(2)}) async-start(s8[13107200]{0:T(1024)(128)(4,1)} %bitcast.46), calls=%async_computation.9 | async-start | bytes 1048576
  66.4 22.6 %collective-permute-start = (bf16[8,64,640]{2,1,0:T(8,128)(2,1)S(1)}, bf16[8,64,640]{2,1,0:T(8,128)(2,1)S(1)}, u32[]{:S(2)}, u32[]{:S(2)}) collective-permute-start(bf16[8,64,640]{2,1,0:T(8,128)(2,1)S(1)} %get-tuple-element.328), channel_id=1, source_target_pairs={{0,4},{4,8},{8,12},{12,16},{16,20},{20,24},{24,28},{28,0},{1,5},{5... | collective-permute-start | bytes 1966088 | tf_op jit(solution)/shard_map/while/body/eval_jaxpr/ppermute | solution.py:11
  67.8 18.8 %collective-permute-start.1 = (s32[32,640]{1,0:T(8,128)S(1)}, s32[32,640]{1,0:T(8,128)S(1)}, u32[]{:S(2)}, u32[]{:S(2)}) collective-permute-start(s32[32,640]{1,0:T(8,128)S(1)} %get-tuple-element.329), channel_id=1, source_target_pairs={{0,4},{4,8},{8,12},{12,16},{16,20},{20,24},{24,28},{28,0},{1,5},{5... | collective-permute-start | bytes 245768 | tf_op jit(solution)/shard_map/while/body/eval_jaxpr/ppermute | solution.py:11
  106.5 21.7 %collective-permute-start = (bf16[8,64,640]{2,1,0:T(8,128)(2,1)S(1)}, bf16[8,64,640]{2,1,0:T(8,128)(2,1)S(1)}, u32[]{:S(2)}, u32[]{:S(2)}) collective-permute-start(bf16[8,64,640]{2,1,0:T(8,128)(2,1)S(1)} %get-tuple-element.328), channel_id=1, source_target_pairs={{0,4},{4,8},{8,12},{12,16},{16,20},{20,24},{24,28},{28,0},{1,5},{5... | collective-permute-start | bytes 1966088 | tf_op jit(solution)/shard_map/while/body/eval_jaxpr/ppermute | solution.py:11
  106.6 19.2 %collective-permute-start.1 = (s32[32,640]{1,0:T(8,128)S(1)}, s32[32,640]{1,0:T(8,128)S(1)}, u32[]{:S(2)}, u32[]{:S(2)}) collective-permute-start(s32[32,640]{1,0:T(8,128)S(1)} %get-tuple-element.329), channel_id=1, source_target_pairs={{0,4},{4,8},{8,12},{12,16},{16,20},{20,24},{24,28},{28,0},{1,5},{5... | collective-permute-start | bytes 245768 | tf_op jit(solution)/shard_map/while/body/eval_jaxpr/ppermute | solution.py:11
  145.7 20.7 %collective-permute-start = (bf16[8,64,640]{2,1,0:T(8,128)(2,1)S(1)}, bf16[8,64,640]{2,1,0:T(8,128)(2,1)S(1)}, u32[]{:S(2)}, u32[]{:S(2)}) collective-permute-start(bf16[8,64,640]{2,1,0:T(8,128)(2,1)S(1)} %get-tuple-element.328), channel_id=1, source_target_pairs={{0,4},{4,8},{8,12},{12,16},{16,20},{20,24},{24,28},{28,0},{1,5},{5... | collective-permute-start | bytes 1966088 | tf_op jit(solution)/shard_map/while/body/eval_jaxpr/ppermute | solution.py:11
  145.8 18.3 %collective-permute-start.1 = (s32[32,640]{1,0:T(8,128)S(1)}, s32[32,640]{1,0:T(8,128)S(1)}, u32[]{:S(2)}, u32[]{:S(2)}) collective-permute-start(s32[32,640]{1,0:T(8,128)S(1)} %get-tuple-element.329), channel_id=1, source_target_pairs={{0,4},{4,8},{8,12},{12,16},{16,20},{20,24},{24,28},{28,0},{1,5},{5... | collective-permute-start | bytes 245768 | tf_op jit(solution)/shard_map/while/body/eval_jaxpr/ppermute | solution.py:11
  183.9 19.8 %collective-permute-start = (bf16[8,64,640]{2,1,0:T(8,128)(2,1)S(1)}, bf16[8,64,640]{2,1,0:T(8,128)(2,1)S(1)}, u32[]{:S(2)}, u32[]{:S(2)}) collective-permute-start(bf16[8,64,640]{2,1,0:T(8,128)(2,1)S(1)} %get-tuple-element.328), channel_id=1, source_target_pairs={{0,4},{4,8},{8,12},{12,16},{16,20},{20,24},{24,28},{28,0},{1,5},{5... | collective-permute-start | bytes 1966088 | tf_op jit(solution)/shard_map/while/body/eval_jaxpr/ppermute | solution.py:11
  183.9 17.4 %collective-permute-start.1 = (s32[32,640]{1,0:T(8,128)S(1)}, s32[32,640]{1,0:T(8,128)S(1)}, u32[]{:S(2)}, u32[]{:S(2)}) collective-permute-start(s32[32,640]{1,0:T(8,128)S(1)} %get-tuple-element.329), channel_id=1, source_target_pairs={{0,4},{4,8},{8,12},{12,16},{16,20},{20,24},{24,28},{28,0},{1,5},{5... | collective-permute-start | bytes 245768 | tf_op jit(solution)/shard_map/while/body/eval_jaxpr/ppermute | solution.py:11
  221.1 18.9 %collective-permute-start = (bf16[8,64,640]{2,1,0:T(8,128)(2,1)S(1)}, bf16[8,64,640]{2,1,0:T(8,128)(2,1)S(1)}, u32[]{:S(2)}, u32[]{:S(2)}) collective-permute-start(bf16[8,64,640]{2,1,0:T(8,128)(2,1)S(1)} %get-tuple-element.328), channel_id=1, source_target_pairs={{0,4},{4,8},{8,12},{12,16},{16,20},{20,24},{24,28},{28,0},{1,5},{5... | collective-permute-start | bytes 1966088 | tf_op jit(solution)/shard_map/while/body/eval_jaxpr/ppermute | solution.py:11
  221.2 16.4 %collective-permute-start.1 = (s32[32,640]{1,0:T(8,128)S(1)}, s32[32,640]{1,0:T(8,128)S(1)}, u32[]{:S(2)}, u32[]{:S(2)}) collective-permute-start(s32[32,640]{1,0:T(8,128)S(1)} %get-tuple-element.329), channel_id=1, source_target_pairs={{0,4},{4,8},{8,12},{12,16},{16,20},{20,24},{24,28},{28,0},{1,5},{5... | collective-permute-start | bytes 245768 | tf_op jit(solution)/shard_map/while/body/eval_jaxpr/ppermute | solution.py:11
  257.6 18.0 %collective-permute-start = (bf16[8,64,640]{2,1,0:T(8,128)(2,1)S(1)}, bf16[8,64,640]{2,1,0:T(8,128)(2,1)S(1)}, u32[]{:S(2)}, u32[]{:S(2)}) collective-permute-start(bf16[8,64,640]{2,1,0:T(8,128)(2,1)S(1)} %get-tuple-element.328), channel_id=1, source_target_pairs={{0,4},{4,8},{8,12},{12,16},{16,20},{20,24},{24,28},{28,0},{1,5},{5... | collective-permute-start | bytes 1966088 | tf_op jit(solution)/shard_map/while/body/eval_jaxpr/ppermute | solution.py:11
  257.6 15.5 %collective-permute-start.1 = (s32[32,640]{1,0:T(8,128)S(1)}, s32[32,640]{1,0:T(8,128)S(1)}, u32[]{:S(2)}, u32[]{:S(2)}) collective-permute-start(s32[32,640]{1,0:T(8,128)S(1)} %get-tuple-element.329), channel_id=1, source_target_pairs={{0,4},{4,8},{8,12},{12,16},{16,20},{20,24},{24,28},{28,0},{1,5},{5... | collective-permute-start | bytes 245768 | tf_op jit(solution)/shard_map/while/body/eval_jaxpr/ppermute | solution.py:11
  293.0 17.1 %collective-permute-start = (bf16[8,64,640]{2,1,0:T(8,128)(2,1)S(1)}, bf16[8,64,640]{2,1,0:T(8,128)(2,1)S(1)}, u32[]{:S(2)}, u32[]{:S(2)}) collective-permute-start(bf16[8,64,640]{2,1,0:T(8,128)(2,1)S(1)} %get-tuple-element.328), channel_id=1, source_target_pairs={{0,4},{4,8},{8,12},{12,16},{16,20},{20,24},{24,28},{28,0},{1,5},{5... | collective-permute-start | bytes 1966088 | tf_op jit(solution)/shard_map/while/body/eval_jaxpr/ppermute | solution.py:11
  293.1 14.6 %collective-permute-start.1 = (s32[32,640]{1,0:T(8,128)S(1)}, s32[32,640]{1,0:T(8,128)S(1)}, u32[]{:S(2)}, u32[]{:S(2)}) collective-permute-start(s32[32,640]{1,0:T(8,128)S(1)} %get-tuple-element.329), channel_id=1, source_target_pairs={{0,4},{4,8},{8,12},{12,16},{16,20},{20,24},{24,28},{28,0},{1,5},{5... | collective-permute-start | bytes 245768 | tf_op jit(solution)/shard_map/while/body/eval_jaxpr/ppermute | solution.py:11
  337.1 422.4 %reduce-scatter.8.cloned.1.call-start = ((), (), s32[]{:S(2)}) async-start(), calls=%async_computation.5 | async-start | bytes 65536000 | tf_op jit(solution)/shard_map/reduce_scatter | solution.py:60
  337.9 781.1 %reduce-scatter.4.cloned.1.call-start = ((), (), s32[]{:S(2)}) async-start(), calls=%async_computation.3 | async-start | bytes 65536000 | tf_op jit(solution)/shard_map/reduce_scatter | solution.py:57
  1125.8 9.2 copy-start
Sparse Core Ops, SparseCore 0:
  337.2 62.6 reduce-scatter.5
  402.7 356.7 reduce-scatter.7
  762.1 356.8 reduce-scatter.3
where the time goes:
time: 1180 us
  waiting for transfers between devices  875 us (74%)
  local copies, waits for them, and re-layouts  156 us (13%)
  matrix products  73.9 us (6%)
  other arithmetic  52.5 us (4%)
  between operations  13.8 us (1%)
    reduce_scatter x1, waiting for transfers between devices, on_device(): lax.psum_scatter(parts[1].astype(jnp.bfloat16), 'win', scatter_dimension=...  355 us
    reduce_scatter x1, waiting for transfers between devices, on_device(): lax.psum_scatter(parts[0].astype(jnp.bfloat16), 'win', scatter_dimension=...  339 us
    ppermute x14, waiting for transfers between devices, shifted(): lax.ppermute(array, axis, [(i, (i + by) % count) for i in range(count)])  118 us
    dynamic_update_slice x8, local copies, waits for them, and re-layouts, accumulate(): lax.dynamic_update_index_in_dim(parts[1], product[:, width:], source, 0)  77.3 us
    reduce_scatter x1, waiting for transfers between devices, on_device(): lax.psum_scatter(parts[2].astype(jnp.bfloat16), 'win', scatter_dimension=...  61.3 us
    dot_general x8, matrix products, accumulate(): jnp.einsum('fwk,fwc->fkc', left, data, preferred_element_type=jnp.float32)  54.8 us
    another operation x2, local copies, waits for them, and re-layouts  36 us
    div x1, other arithmetic, on_device(): return (flat_re / denom, flat_im / denom)  34.2 us
  transfers between devices with their start and end apart: 17, of which 10 were waited for; matrix products, arithmetic and copies ran while one was open for 4% of the time, Pallas kernels for 0%

commit v1 on v0

v1 whole, which is shorter than its diff:
```python
import functools

import jax
import jax.numpy as jnp
from jax import lax
from jax.experimental import pallas as pl
from jax.experimental.pallas import tpu as pltpu
from jax.sharding import PartitionSpec as P

water_level = 1.0
MESH = pl.DeviceIdType.MESH


def whitened(real_part, imag_part, mask):
    real_part = real_part.astype(jnp.float32)
    imag_part = imag_part.astype(jnp.float32)
    power = real_part * real_part + imag_part * imag_part
    factor = mask * lax.rsqrt(jnp.maximum(power, water_level * water_level))
    return (real_part * factor).astype(jnp.bfloat16), (imag_part * factor).astype(jnp.bfloat16)


def gather_kernel(bins, wins, pieces, planes,
                  re_ref, im_ref, valid_ref, rows, cols, relay, own,
                  core_s, core_r, xrow_s, xrow_r, pair_s, pair_r,
                  up_p, dn_p, zp_r, up_q, dn_q, zq_r, x_s, x_r, y_s, y_r, local_s):
    c = lax.axis_index("chan")
    w = lax.axis_index("win")
    z, y = c // 2, c % 2
    core = w % 2
    plane, other = w, (w + 2) % 4
    mate = w + 1 - 2 * core
    s0 = (w, mate)
    s1 = ((w + 2) % 4, (mate + 2) % 4)
    dev_core = (c, mate)
    dev_x = (c, (w + 2) % 4)
    dev_y = (c + 1 - 2 * y, w)
    dev_up = (jnp.minimum(c + 2, 2 * planes - 1), w)
    dev_dn = (jnp.maximum(c - 2, 0), w)
    has_up, has_dn = z < planes - 1, z > 0

    barrier = pltpu.get_barrier_semaphore()
    for dev in (dev_core, dev_x, dev_y):
        pl.semaphore_signal(barrier, inc=1, device_id=dev, device_id_type=MESH)

    @pl.when(has_up)
    def _():
        pl.semaphore_signal(barrier, inc=1, device_id=dev_up, device_id_type=MESH)

    @pl.when(has_dn)
    def _():
        pl.semaphore_signal(barrier, inc=1, device_id=dev_dn, device_id_type=MESH)

    peers = 3 + has_up.astype(jnp.int32) + has_dn.astype(jnp.int32)
    pl.semaphore_wait(barrier, peers)

    depth = 2 * wins
    per = bins // pieces
    cuts = []
    for i in range(pieces):
        size = per * depth + (wins if i == pieces - 1 else 0)
        cuts.append(pl.ds(i * per * depth, size))

    sent = []

    def send(src, dst, ssem, rsem, dev, cond=None):
        def make():
            return pltpu.make_async_remote_copy(
                src_ref=src, dst_ref=dst, send_sem=ssem, recv_sem=rsem,
                device_id=dev, device_id_type=MESH)
        if cond is None:
            make().start()
        else:
            @pl.when(cond)
            def _():
                make().start()
        sent.append((make, cond))

    def arrive(dst, ssem, rsem):
        pltpu.make_async_remote_copy(
            src_ref=dst, dst_ref=dst, send_sem=ssem, recv_sem=rsem,
            device_id=dev_core, device_id_type=MESH).wait_recv()

    is_p, is_q = z == plane, z == other
    go_up_p = (z >= plane) & has_up
    go_dn_p = (z <= plane) & has_dn
    go_up_q = (z >= other) & has_up
    go_dn_q = (z <= other) & has_dn

    def along(i, u, kk, src, cond_at, into_p):
        cut = cuts[i]
        if into_p:
            dst = cols.at[y, s0[kk], cut]
            send(src, dst, up_p.at[u], zp_r.at[u], dev_up, cond_at & go_up_p)
            send(src, dst, dn_p.at[u], zp_r.at[u], dev_dn, cond_at & go_dn_p)
        else:
            dst = relay.at[kk, cut]
            send(src, dst, up_q.at[u], zq_r.at[u], dev_up, cond_at & go_up_q)
            send(src, dst, dn_q.at[u], zq_r.at[u], dev_dn, cond_at & go_dn_q)

    def source(i, kk, src):
        u = kk * pieces + i
        along(i, u, kk, src, is_p, True)
        along(i, u, kk, src, is_q, False)
        send(src, cols.at[y, s0[kk], cuts[i]], y_s.at[u], y_r.at[u], dev_y, is_p)

    mask = valid_ref[...].astype(jnp.float32)
    locals_ = []
    for i in range(pieces):
        for f in range(i * per, (i + 1) * per):
            wr, wi = whitened(re_ref[f], im_ref[f], mask)
            own[pl.ds(f * depth, wins), :] = wr
            own[pl.ds(f * depth + wins, wins), :] = wi
        if i == pieces - 1:
            own[pl.ds(bins * depth, wins), :] = mask.astype(jnp.bfloat16)
        src = own.at[cuts[i]]
        send(src, rows.at[w, cuts[i]], core_s.at[i], core_r.at[i], dev_core)
        source(i, 0, src)
        send(src, rows.at[w, cuts[i]], xrow_s.at[i], xrow_r.at[i], dev_x)
        copy = pltpu.make_async_copy(src, rows.at[w, cuts[i]], local_s.at[i])
        copy.start()
        locals_.append(copy)

    half = 2 * pieces
    for kk in range(2):
        for i in range(pieces):
            cut = cuts[i]
            u = kk * pieces + i
            if kk == 0:
                arrive(rows.at[mate, cut], core_s.at[i], core_r.at[i])
                source(i, 1, rows.at[mate, cut])

            @pl.when(jnp.logical_not(is_p))
            def _():
                arrive(cols.at[y, s0[kk], cut], up_p.at[u], zp_r.at[u])

            here = cols.at[y, s0[kk], cut]
            along(i, u, kk, here, jnp.logical_not(is_p), True)
            send(here, here, y_s.at[u], y_r.at[u], dev_y, jnp.logical_not(is_p))

            @pl.when(jnp.logical_not(is_q))
            def _():
                arrive(relay.at[kk, cut], up_q.at[u], zq_r.at[u])

            here = relay.at[kk, cut]
            along(i, u, kk, here, jnp.logical_not(is_q), False)
            send(here, cols.at[y, s0[kk], cut], x_s.at[u], x_r.at[u], dev_x, jnp.logical_not(is_q))

            here = rows.at[s1[kk], cut]
            if kk == 0:
                arrive(here, xrow_s.at[i], xrow_r.at[i])
                send(here, here, pair_s.at[i], pair_r.at[i], dev_core)
            else:
                arrive(here, pair_s.at[i], pair_r.at[i])
            send(here, cols.at[y, s1[kk], cut], y_s.at[half + u], y_r.at[half + u], dev_y, is_p)

            @pl.when(jnp.logical_not(is_p))
            def _():
                arrive(cols.at[y, s1[kk], cut], x_s.at[u], x_r.at[u])

            here = cols.at[y, s1[kk], cut]
            send(here, here, y_s.at[half + u], y_r.at[half + u], dev_y, jnp.logical_not(is_p))

    for copy in locals_:
        copy.wait()

    @pl.when(is_p)
    def _():
        copy = pltpu.make_async_copy(rows, cols.at[y], local_s.at[pieces])
        copy.start()
        copy.wait()

    for kk in range(2):
        for i in range(pieces):
            u = kk * pieces + i
            arrive(cols.at[1 - y, s0[kk], cuts[i]], y_s.at[u], y_r.at[u])
            arrive(cols.at[1 - y, s1[kk], cuts[i]], y_s.at[half + u], y_r.at[half + u])

    for make, cond in sent:
        if cond is None:
            make().wait_send()
        else:
            @pl.when(cond)
            def _(make=make):
                make().wait_send()


def gather_call(spec_re, spec_im, valid, planes):
    bins, wins, width = spec_re.shape
    pieces = 4
    deep = bins * 2 * wins + wins
    sems = lambda n: pltpu.SemaphoreType.DMA((n,))
    u = 2 * pieces
    return pl.pallas_call(
        functools.partial(gather_kernel, bins, wins, pieces, planes),
        out_shape=[
            jax.ShapeDtypeStruct((4, deep, width), jnp.bfloat16),
            jax.ShapeDtypeStruct((2, 4, deep, width), jnp.bfloat16),
            jax.ShapeDtypeStruct((2, deep, width), jnp.bfloat16),
        ],
        in_specs=[pl.BlockSpec(memory_space=pltpu.VMEM)] * 3,
        out_specs=[pl.BlockSpec(memory_space=pl.ANY)] * 3,
        scratch_shapes=[
            pltpu.VMEM((deep, width), jnp.bfloat16),
            sems(pieces), sems(pieces), sems(pieces), sems(pieces), sems(pieces), sems(pieces),
            sems(u), sems(u), sems(u), sems(u), sems(u), sems(u),
            sems(u), sems(u), sems(2 * u), sems(2 * u), sems(pieces + 1),
        ],
        compiler_params=pltpu.CompilerParams(
            collective_id=0, has_side_effects=True, vmem_limit_bytes=16 * 2**20),
    )(spec_re, spec_im, valid)


def spectra_kernel(row_ref, row_mask_ref, col_ref, col_mask_ref, re_ref, im_ref, left_re, left_im, scale):
    f, h = pl.program_id(0), pl.program_id(1)
    wins = row_mask_ref.shape[1]
    width = row_ref.shape[2]
    groups = row_ref.shape[0]

    @pl.when(h == 0)
    def _():
        block = row_ref[...]
        real_part, imag_part = block[:, :wins], block[:, wins:]
        depth = groups * 2 * wins
        left_re[...] = block.reshape(depth, width).T
        left_im[...] = jnp.concatenate([imag_part, -real_part], 1).reshape(depth, width).T

    @pl.when(f == 0)
    def _():
        rows_mask = row_mask_ref[...].reshape(groups * wins, width)
        cols_mask = col_mask_ref[0].reshape(groups * wins, width)
        count = lax.dot_general(rows_mask, cols_mask, (((0,), (0,)), ((), ())),
                                preferred_element_type=jnp.float32)
        scale[h] = 1.0 / jnp.maximum(count, 1.0)

    right = col_ref[0].reshape(groups * 2 * wins, width)
    re_ref[0] = jnp.dot(left_re[...], right, preferred_element_type=jnp.float32) * scale[h]
    im_ref[0] = jnp.dot(left_im[...], right, preferred_element_type=jnp.float32) * scale[h]


def spectra_call(rows, cols, bins, wins):
    groups, _, width = rows.shape
    halves = cols.shape[0]
    depth = groups * 2 * wins
    out = jax.ShapeDtypeStruct((bins, width, halves * width), jnp.float32)
    last = 2 * bins
    return pl.pallas_call(
        spectra_kernel,
        grid=(bins, halves),
        out_shape=[out, out],
        in_specs=[
            pl.BlockSpec((groups, 2 * wins, width), lambda f, h: (0, f, 0)),
            pl.BlockSpec((groups, wins, width), lambda f, h: (0, last, 0)),
            pl.BlockSpec((1, groups, 2 * wins, width), lambda f, h: (h, 0, f, 0)),
            pl.BlockSpec((1, groups, wins, width), lambda f, h: (h, 0, last, 0)),
        ],
        out_specs=[pl.BlockSpec((1, width, width), lambda f, h: (f, 0, h))] * 2,
        scratch_shapes=[
            pltpu.VMEM((width, depth), jnp.bfloat16),
            pltpu.VMEM((width, depth), jnp.bfloat16),
            pltpu.VMEM((halves, width, width), jnp.float32),
        ],
        compiler_params=pltpu.CompilerParams(vmem_limit_bytes=28 * 2**20),
    )(rows, rows, cols, cols)


def on_device_kernels(spec_re, spec_im, valid):
    bins, wins, _ = spec_re.shape
    rows, cols, _ = gather_call(spec_re, spec_im, valid, lax.axis_size("chan") // 2)
    return tuple(spectra_call(rows, cols, bins, wins))


def on_device_general(spec_re, spec_im, valid):
    bins, wins, width = spec_re.shape
    mask = valid.astype(jnp.float32)
    white_re, white_im = whitened(spec_re, spec_im, mask[None])
    mine = jnp.concatenate(
        [white_re.reshape(bins * wins, width), white_im.reshape(bins * wins, width),
         mask.astype(jnp.bfloat16)], 0)
    rows = lax.all_gather(mine, "win")
    groups = rows.shape[0]
    every = lax.all_gather(rows, "chan")
    blocks = every.shape[0] // groups
    cols = lax.dynamic_slice_in_dim(every, lax.axis_index("win") * blocks, blocks, 0)
    cols = jnp.transpose(cols, (1, 2, 0, 3)).reshape(groups, rows.shape[1], blocks * width)

    def split(array):
        n = array.shape[2]
        size = bins * wins
        return (array[:, :size].reshape(groups, bins, wins, n),
                array[:, size:2 * size].reshape(groups, bins, wins, n), array[:, 2 * size:])

    row_re, row_im, row_mask = split(rows)
    col_re, col_im, col_mask = split(cols)
    right = jnp.concatenate([col_re, col_im], 2)

    def product(left):
        return jnp.einsum("gfwi,gfwj->fij", left, right, preferred_element_type=jnp.float32)

    count = jnp.einsum("gwi,gwj->ij", row_mask, col_mask, preferred_element_type=jnp.float32)
    denom = jnp.maximum(count, 1.0)[None]
    total_re = product(jnp.concatenate([row_re, row_im], 2))
    total_im = product(jnp.concatenate([row_im, -row_re], 2))
    return (total_re / denom, total_im / denom)


def solution(mesh):
    fits = mesh.shape["chan"] == 8 and mesh.shape["win"] == 4
    on_device = on_device_kernels if fits else on_device_general
    in_specs = (P(None, "win", "chan"), P(None, "win", "chan"), P("win", "chan"))
    out_specs = (P(None, "chan", "win"), P(None, "chan", "win"))
    return jax.shard_map(
        on_device, mesh=mesh, in_specs=in_specs, out_specs=out_specs, check_vma=False
    )
```

time: 1180 us -> 109 us (0.09)
  waiting for transfers between devices: 875 us -> 0 us
  local copies, waits for them, and re-layouts: 156 us -> 2.82 us
  Pallas kernels: 0 us -> 106 us
  matrix products: 73.9 us -> 0 us
  other arithmetic: 52.5 us -> 0 us
  between operations: 13.8 us -> 0.65 us
    reduce_scatter x3 -> x0, waiting for transfers between devices: 755 us -> none  [the longest x1 355 us: on_device(): lax.psum_scatter(parts[1].astype(jnp.bfloat16), 'win', scatter_dimension=...]
    ppermute x14 -> x0, waiting for transfers between devices: 118 us -> none  [shifted(): lax.ppermute(array, axis, [(i, (i + by) % count) for i in range(count)])]
    pallas_call x0 -> x2, Pallas kernels: none -> 106 us  [the longest x1 84.4 us: gather_call(): pl.pallas_call(functools.partial(gather_kernel, bins, wins, pieces, plane...]
    dynamic_update_slice x9 -> x0, local copies, waits for them, and re-layouts: 80.6 us -> none  [the longest x8 77.3 us: accumulate(): lax.dynamic_update_index_in_dim(parts[1], product[:, width:], source, 0)]
    dot_general x16 -> x0, matrix products: 73.9 us -> none  [the longest x8 54.8 us: accumulate(): jnp.einsum('fwk,fwc->fkc', left, data, preferred_element_type=jnp.float32)]
    another operation x2 -> x0, local copies, waits for them, and re-layouts: 36 us -> none
    div x1 -> x0, other arithmetic: 34.2 us -> none  [on_device(): return (flat_re / denom, flat_im / denom)]
    reshape x2 -> x0, local copies, waits for them, and re-layouts: 22.7 us -> none  [the longest x1 13.6 us: on_device(): jnp.transpose(summed_im, (1, 2, 0, 3)).reshape(bins, width, owned * width)]
  transfers between devices with their start and end apart: 17 -> 0, of which waited for: 10 -> 0; matrix products, arithmetic and copies ran while one was open for 4% -> 0% of each run, Pallas kernels for 0% -> 0%
where the time goes in v1:
time: 109 us
  Pallas kernels  106 us (97%)
  local copies, waits for them, and re-layouts  2.82 us (3%)
    pallas_call x1, Pallas kernels, gather_call(): pl.pallas_call(functools.partial(gather_kernel, bins, wins, pieces, plane...  84.4 us
    pallas_call x1, Pallas kernels, spectra_call(): pl.pallas_call(spectra_kernel, grid=(bins, halves), out_shape=[out, out],...  21.3 us
    unnamed x6, local copies, waits for them, and re-layouts  2.82 us

profile of v1, /device:TPU:3, one launch (start us, length us, event | category | flops | bytes accessed | tf_op | source)
XLA Modules:
  0.0 109.2 jit_solution(6921627296898577485)
XLA Ops:
  0.6 0.0 copy-start
  0.6 1.0 copy-done
  1.6 0.0 copy-start.1
  1.6 1.0 copy-done.1
  2.6 0.0 copy-start.2
  2.6 0.9 copy-done.2
  3.5 84.4 %shard_map.50 = (bf16[4,544,640]{2,1,0:T(8,128)(2,1)S(1)}, bf16[2,4,544,640]{3,2,1,0:T(8,128)(2,1)S(1)}, bf16[2,544,640]{2,1,0:T(8,128)(2,1)}) custom-call(bf16[8,32,640]{2,1,0:T(8,128)(2,1)S(1)} %copy-done, bf16[8,32,640]{2,1,0:T(8,128)(2,1)S(1)} %copy-done.1, s32[32,640]{1,0:T(8,128)S(1)} %copy-done.2), custom_call_target="tpu_custom_call" | custom-call | tf_op jit(solution)/shard_map/pallas_call | solution.py:193
  87.8 21.3 %shard_map.51 = (f32[8,640,1280]{2,1,0:T(8,128)}, f32[8,640,1280]{2,1,0:T(8,128)}) custom-call(bf16[4,544,640]{2,1,0:T(8,128)(2,1)S(1)} %get-tuple-element.4.row_ref.row_mask_ref, bf16[4,544,640]{2,1,0:T(8,128)(2,1)S(1)} %get-tuple-element.4.row_ref.row_mask_ref, bf16[2,4,544,640]{3,2,1,0:T(8,128)(2,1)S(1)} %get-tuple-element.5.col_ref.col_mask_ref, ...), custom_call_target="tpu_custom_call" | custom-call | tf_op jit(solution)/shard_map/pallas_call | solution.py:246
Async XLA Ops:
  0.6 1.0 copy-start
  1.6 1.0 copy-start.1
  2.6 0.9 copy-start.2

commit v2 on v1

--- a/solution.py
+++ b/solution.py
@@ -20,7 +20,7 @@
 
 
 def gather_kernel(bins, wins, pieces, planes,
-                  re_ref, im_ref, valid_ref, rows, cols, relay, own,
+                  re_hbm, im_hbm, valid_hbm, rows, cols, relay, re_ref, im_ref, valid_ref, own, input_s,
                   core_s, core_r, xrow_s, xrow_r, pair_s, pair_r,
                   up_p, dn_p, zp_r, up_q, dn_q, zq_r, x_s, x_r, y_s, y_r, local_s):
     c = lax.axis_index("chan")
@@ -38,6 +38,11 @@
     dev_dn = (jnp.maximum(c - 2, 0), w)
     has_up, has_dn = z < planes - 1, z > 0
 
+    loads = [pltpu.make_async_copy(src, dst, input_s.at[n]) for n, (src, dst) in enumerate(
+        ((re_hbm, re_ref), (im_hbm, im_ref), (valid_hbm, valid_ref)))]
+    for load in loads:
+        load.start()
+
     barrier = pltpu.get_barrier_semaphore()
     for dev in (dev_core, dev_x, dev_y):
         pl.semaphore_signal(barrier, inc=1, device_id=dev, device_id_type=MESH)
@@ -75,6 +80,17 @@
                 make().start()
         sent.append((make, cond))
 
+    def settle(first, last):
+        for n in range(first, last):
+            if sent[n] is not None:
+                make, cond = sent[n]
+
+                @pl.when(cond)
+                def _():
+                    make().wait_send()
+
+                sent[n] = None
+
     def arrive(dst, ssem, rsem):
         pltpu.make_async_remote_copy(
             src_ref=dst, dst_ref=dst, send_sem=ssem, recv_sem=rsem,
@@ -97,14 +113,34 @@
             send(src, dst, up_q.at[u], zq_r.at[u], dev_up, cond_at & go_up_q)
             send(src, dst, dn_q.at[u], zq_r.at[u], dev_dn, cond_at & go_dn_q)
 
+    late_up, late_dn = z == planes - 2, z == 1
+
+    def source_z(i, kk, src, late):
+        u = kk * pieces + i
+        cut = cuts[i]
+        to_up = has_up & (late_up if late else jnp.logical_not(late_up))
+        to_dn = has_dn & (late_dn if late else jnp.logical_not(late_dn))
+        dst = cols.at[y, s0[kk], cut]
+        send(src, dst, up_p.at[u], zp_r.at[u], dev_up, is_p & to_up)
+        send(src, dst, dn_p.at[u], zp_r.at[u], dev_dn, is_p & to_dn)
+        dst = relay.at[kk, cut]
+        send(src, dst, up_q.at[u], zq_r.at[u], dev_up, is_q & to_up)
+        send(src, dst, dn_q.at[u], zq_r.at[u], dev_dn, is_q & to_dn)
+
     def source(i, kk, src):
         u = kk * pieces + i
-        along(i, u, kk, src, is_p, True)
-        along(i, u, kk, src, is_q, False)
+        source_z(i, kk, src, False)
         send(src, cols.at[y, s0[kk], cuts[i]], y_s.at[u], y_r.at[u], dev_y, is_p)
 
+    rows_first_out = (z // 2) == 1 - w // 2
+    rows_first_in = (z // 2) == w // 2
+
+    for load in loads:
+        load.wait()
     mask = valid_ref[...].astype(jnp.float32)
     locals_ = []
+    marks = []
+    lag = 1
     for i in range(pieces):
         for f in range(i * per, (i + 1) * per):
             wr, wi = whitened(re_ref[f], im_ref[f], mask)
@@ -113,9 +149,13 @@
         if i == pieces - 1:
             own[pl.ds(bins * depth, wins), :] = mask.astype(jnp.bfloat16)
         src = own.at[cuts[i]]
+        if i >= lag:
+            settle(*marks[i - lag])
         send(src, rows.at[w, cuts[i]], core_s.at[i], core_r.at[i], dev_core)
+        first = len(sent)
         source(i, 0, src)
-        send(src, rows.at[w, cuts[i]], xrow_s.at[i], xrow_r.at[i], dev_x)
+        marks.append((first, first + 4))
+        send(src, rows.at[w, cuts[i]], xrow_s.at[i], xrow_r.at[i], dev_x, rows_first_out)
         copy = pltpu.make_async_copy(src, rows.at[w, cuts[i]], local_s.at[i])
         copy.start()
         locals_.append(copy)
@@ -145,12 +185,30 @@
             along(i, u, kk, here, jnp.logical_not(is_q), False)
             send(here, cols.at[y, s0[kk], cut], x_s.at[u], x_r.at[u], dev_x, jnp.logical_not(is_q))
 
-            here = rows.at[s1[kk], cut]
+            source_z(i, kk, own.at[cut] if kk == 0 else rows.at[mate, cut], True)
+            later = jnp.logical_not(rows_first_in)
+            first_row, pair_row = rows.at[s1[0], cut], rows.at[s1[1], cut]
             if kk == 0:
-                arrive(here, xrow_s.at[i], xrow_r.at[i])
-                send(here, here, pair_s.at[i], pair_r.at[i], dev_core)
+                send(own.at[cut], rows.at[w, cut], xrow_s.at[i], xrow_r.at[i], dev_x,
+                     jnp.logical_not(rows_first_out))
+
+                @pl.when(rows_first_in)
+                def _():
+                    arrive(first_row, xrow_s.at[i], xrow_r.at[i])
+
+                send(first_row, first_row, pair_s.at[i], pair_r.at[i], dev_core, rows_first_in)
+                here = first_row
             else:
-                arrive(here, pair_s.at[i], pair_r.at[i])
+                @pl.when(rows_first_in)
+                def _():
+                    arrive(pair_row, pair_s.at[i], pair_r.at[i])
+
+                @pl.when(later)
+                def _():
+                    arrive(first_row, xrow_s.at[i], xrow_r.at[i])
+
+                send(first_row, first_row, pair_s.at[i], pair_r.at[i], dev_core, later)
+                here = pair_row
             send(here, cols.at[y, s1[kk], cut], y_s.at[half + u], y_r.at[half + u], dev_y, is_p)
 
             @pl.when(jnp.logical_not(is_p))
@@ -168,6 +226,11 @@
         copy = pltpu.make_async_copy(rows, cols.at[y], local_s.at[pieces])
         copy.start()
         copy.wait()
+
+    for i in range(pieces):
+        @pl.when(jnp.logical_not(rows_first_in))
+        def _(i=i):
+            arrive(rows.at[s1[1], cuts[i]], pair_s.at[i], pair_r.at[i])
 
     for kk in range(2):
         for i in range(pieces):
@@ -175,7 +238,10 @@
             arrive(cols.at[1 - y, s0[kk], cuts[i]], y_s.at[u], y_r.at[u])
             arrive(cols.at[1 - y, s1[kk], cuts[i]], y_s.at[half + u], y_r.at[half + u])
 
-    for make, cond in sent:
+    for entry in sent:
+        if entry is None:
+            continue
+        make, cond = entry
         if cond is None:
             make().wait_send()
         else:
@@ -186,7 +252,7 @@
 
 def gather_call(spec_re, spec_im, valid, planes):
     bins, wins, width = spec_re.shape
-    pieces = 4
+    pieces = bins // 2
     deep = bins * 2 * wins + wins
     sems = lambda n: pltpu.SemaphoreType.DMA((n,))
     u = 2 * pieces
@@ -197,10 +263,14 @@
             jax.ShapeDtypeStruct((2, 4, deep, width), jnp.bfloat16),
             jax.ShapeDtypeStruct((2, deep, width), jnp.bfloat16),
         ],
-        in_specs=[pl.BlockSpec(memory_space=pltpu.VMEM)] * 3,
+        in_specs=[pl.BlockSpec(memory_space=pltpu.HBM)] * 3,
         out_specs=[pl.BlockSpec(memory_space=pl.ANY)] * 3,
         scratch_shapes=[
+            pltpu.VMEM((bins, wins, width), jnp.bfloat16),
+            pltpu.VMEM((bins, wins, width), jnp.bfloat16),
+            pltpu.VMEM((wins, width), jnp.int32),
             pltpu.VMEM((deep, width), jnp.bfloat16),
+            sems(3),
             sems(pieces), sems(pieces), sems(pieces), sems(pieces), sems(pieces), sems(pieces),
             sems(u), sems(u), sems(u), sems(u), sems(u), sems(u),
             sems(u), sems(u), sems(2 * u), sems(2 * u), sems(pieces + 1),
@@ -210,56 +280,64 @@
     )(spec_re, spec_im, valid)
 
 
-def spectra_kernel(row_ref, row_mask_ref, col_ref, col_mask_ref, re_ref, im_ref, left_re, left_im, scale):
-    f, h = pl.program_id(0), pl.program_id(1)
+def spectra_kernel(row_ref, row_mask_ref, col_ref, col_mask_ref, re_ref, im_ref,
+                   left_re, left_im, scale, right):
+    f, t = pl.program_id(0), pl.program_id(1)
     wins = row_mask_ref.shape[1]
-    width = row_ref.shape[2]
-    groups = row_ref.shape[0]
-
-    @pl.when(h == 0)
+    groups, _, width = row_ref.shape
+    halves = col_ref.shape[0]
+    depth = groups * 2 * wins
+
+    @pl.when(t == 0)
     def _():
         block = row_ref[...]
         real_part, imag_part = block[:, :wins], block[:, wins:]
-        depth = groups * 2 * wins
         left_re[...] = block.reshape(depth, width).T
         left_im[...] = jnp.concatenate([imag_part, -real_part], 1).reshape(depth, width).T
-
-    @pl.when(f == 0)
+        for h in range(halves):
+            right[:, h * width:(h + 1) * width] = col_ref[h].reshape(depth, width)
+
+    @pl.when((f == 0) & (t == 0))
     def _():
         rows_mask = row_mask_ref[...].reshape(groups * wins, width)
-        cols_mask = col_mask_ref[0].reshape(groups * wins, width)
-        count = lax.dot_general(rows_mask, cols_mask, (((0,), (0,)), ((), ())),
-                                preferred_element_type=jnp.float32)
-        scale[h] = 1.0 / jnp.maximum(count, 1.0)
-
-    right = col_ref[0].reshape(groups * 2 * wins, width)
-    re_ref[0] = jnp.dot(left_re[...], right, preferred_element_type=jnp.float32) * scale[h]
-    im_ref[0] = jnp.dot(left_im[...], right, preferred_element_type=jnp.float32) * scale[h]
+        for h in range(halves):
+            cols_mask = col_mask_ref[h].reshape(groups * wins, width)
+            count = lax.dot_general(rows_mask, cols_mask, (((0,), (0,)), ((), ())),
+                                    preferred_element_type=jnp.float32)
+            scale[:, h * width:(h + 1) * width] = 1.0 / jnp.maximum(count, 1.0)
+
+    size = re_ref.shape[1]
+    tile = pl.ds(pl.multiple_of(t * size, size), size)
+    block = right[...]
+    re_ref[0] = jnp.dot(left_re[tile], block, preferred_element_type=jnp.float32) * scale[tile]
+    im_ref[0] = jnp.dot(left_im[tile], block, preferred_element_type=jnp.float32) * scale[tile]
 
 
 def spectra_call(rows, cols, bins, wins):
     groups, _, width = rows.shape
     halves = cols.shape[0]
     depth = groups * 2 * wins
+    tiles = 2
     out = jax.ShapeDtypeStruct((bins, width, halves * width), jnp.float32)
     last = 2 * bins
     return pl.pallas_call(
         spectra_kernel,
-        grid=(bins, halves),
+        grid=(bins, tiles),
         out_shape=[out, out],
         in_specs=[
-            pl.BlockSpec((groups, 2 * wins, width), lambda f, h: (0, f, 0)),
-            pl.BlockSpec((groups, wins, width), lambda f, h: (0, last, 0)),
-            pl.BlockSpec((1, groups, 2 * wins, width), lambda f, h: (h, 0, f, 0)),
-            pl.BlockSpec((1, groups, wins, width), lambda f, h: (h, 0, last, 0)),
+            pl.BlockSpec((groups, 2 * wins, width), lambda f, t: (0, f, 0)),
+            pl.BlockSpec((groups, wins, width), lambda f, t: (0, last, 0)),
+            pl.BlockSpec((halves, groups, 2 * wins, width), lambda f, t: (0, 0, f, 0)),
+            pl.BlockSpec((halves, groups, wins, width), lambda f, t: (0, 0, last, 0)),
         ],
-        out_specs=[pl.BlockSpec((1, width, width), lambda f, h: (f, 0, h))] * 2,
+        out_specs=[pl.BlockSpec((1, width // tiles, halves * width), lambda f, t: (f, t, 0))] * 2,
         scratch_shapes=[
             pltpu.VMEM((width, depth), jnp.bfloat16),
             pltpu.VMEM((width, depth), jnp.bfloat16),
-            pltpu.VMEM((halves, width, width), jnp.float32),
+            pltpu.VMEM((width, halves * width), jnp.float32),
+            pltpu.VMEM((depth, halves * width), jnp.bfloat16),
         ],
-        compiler_params=pltpu.CompilerParams(vmem_limit_bytes=28 * 2**20),
+        compiler_params=pltpu.CompilerParams(vmem_limit_bytes=30 * 2**20),
     )(rows, rows, cols, cols)
 
 

time: 109 us -> 108 us (level)
  Pallas kernels: 106 us -> 104 us
where the time goes in v2:
time: 108 us
  Pallas kernels  104 us (96%)
  local copies, waits for them, and re-layouts  2.82 us (3%)
    pallas_call x1, Pallas kernels, gather_call(): pl.pallas_call(functools.partial(gather_kernel, bins, wins, pieces, plane...  84 us
    pallas_call x1, Pallas kernels, spectra_call(): pl.pallas_call(spectra_kernel, grid=(bins, tiles), out_shape=[out, out],...  20.3 us
    unnamed x6, local copies, waits for them, and re-layouts  2.82 us

profile of v2, /device:TPU:3, one launch (start us, length us, event | category | flops | bytes accessed | tf_op | source)
XLA Modules:
  0.0 107.8 jit_solution(14448092241427445769)
XLA Ops:
  0.6 0.0 copy-start
  0.6 1.0 copy-done
  1.6 0.0 copy-start.1
  1.6 1.0 copy-done.1
  2.6 0.0 copy-start.2
  2.6 0.9 copy-done.2
  3.5 84.0 %shard_map.50 = (bf16[4,544,640]{2,1,0:T(8,128)(2,1)S(1)}, bf16[2,4,544,640]{3,2,1,0:T(8,128)(2,1)S(1)}, bf16[2,544,640]{2,1,0:T(8,128)(2,1)}) custom-call(bf16[8,32,640]{2,1,0:T(8,128)(2,1)S(1)} %copy-done, bf16[8,32,640]{2,1,0:T(8,128)(2,1)S(1)} %copy-done.1, s32[32,640]{1,0:T(8,128)S(1)} %copy-done.2), custom_call_target="tpu_custom_call" | custom-call | tf_op jit(solution)/shard_map/pallas_call | solution.py:259
  87.5 20.3 %shard_map.51 = (f32[8,640,1280]{2,1,0:T(8,128)}, f32[8,640,1280]{2,1,0:T(8,128)}) custom-call(bf16[4,544,640]{2,1,0:T(8,128)(2,1)S(1)} %get-tuple-element.4.row_ref.row_mask_ref, bf16[4,544,640]{2,1,0:T(8,128)(2,1)S(1)} %get-tuple-element.4.row_ref.row_mask_ref, bf16[2,4,544,640]{3,2,1,0:T(8,128)(2,1)S(1)} %get-tuple-element.5.col_ref.col_mask_ref, ...), custom_call_target="tpu_custom_call" | custom-call | tf_op jit(solution)/shard_map/pallas_call | solution.py:323
Async XLA Ops:
  0.6 1.0 copy-start
  1.6 1.0 copy-start.1
  2.6 0.9 copy-start.2
